TPU v7x, 128 devices: a whole 4x4x4 slice. The times are simulated.
128 devices in a mesh: dp: 8 (over y, core), ctx: 16 (over z, x).
Axes of the slice: x: 4, y: 4, z: 4, core: 2. Of those that a mesh axis runs over, the one named last changes fastest.
Arguments:
- queries: bfloat16 [8, 2048, 8192], P('dp', 'ctx'), may hold values from -8 to 8
- key_vectors: bfloat16 [8, 2048, 8192], P('dp', 'ctx'), may hold values from -8 to 8
- value_vectors: bfloat16 [8, 2048, 8192], P('dp', 'ctx'), may hold values from -6 to 6
- out_grad: bfloat16 [8, 2048, 8192], P('dp', 'ctx'), may hold values from -6 to 6
- doc_lengths: int32 [8, 16], P('dp'), may hold values from 1 to 384, 2048 in all within a row
Outputs:
- attended: bfloat16 [8, 2048, 8192], P('dp', 'ctx')
- log_totals: float32 [8, 64, 2048], P('dp', None, 'ctx')
- query_grad: bfloat16 [8, 2048, 8192], P('dp', 'ctx')
- key_grad: bfloat16 [8, 2048, 8192], P('dp', 'ctx')
- value_grad: bfloat16 [8, 2048, 8192], P('dp', 'ctx')
Inputs may be any that keep to these rules, and one draw needn't show every extreme that they name: `doc_lengths`: each row of 16 lengths sums to 2048; in every row the largest is exactly 384.
All inputs are finite; a program needn't handle non-finite values.
Results may differ from a plain program's by a relative error of at most 0.024.
Values may be sent and summed in bfloat16 or wider, within the bound.
A program may use at most 256 MiB of HBM per device.

v0:
```python
import jax
import jax.numpy as jnp
from jax import lax
from jax.sharding import PartitionSpec as P

DH = 128
SPAN = 3


def from_behind(block, axis, distance):
    devices = range(lax.axis_size(axis))
    route = [(i - distance, i) for i in devices if i - distance in devices]
    return lax.ppermute(block, axis, route)


def key_mask(lengths, position, rows):
    query_pos = position * rows + jnp.arange(rows, dtype=jnp.int32)
    key_pos = (position - SPAN) * rows + jnp.arange((SPAN + 1) * rows, dtype=jnp.int32)
    starts = jnp.cumsum(lengths, axis=1, dtype=jnp.int32) - lengths
    hit = starts[:, None, :] <= query_pos[None, :, None]
    first = jnp.max(jnp.where(hit, starts[:, None, :], 0), axis=2)
    return (key_pos[None, None, :] >= first[:, :, None]) & (
        key_pos[None, None, :] <= query_pos[None, :, None]
    )


def attend(queries, key_vectors, value_vectors, out_grad, lengths):
    batch, rows, width = queries.shape
    head_count = width // DH
    scale = DH ** (-0.5)
    earlier = [
        from_behind((key_vectors, value_vectors), "ctx", SPAN - offset) for offset in range(SPAN)
    ]
    window = (SPAN + 1) * rows
    key_window = jnp.concatenate([pair[0] for pair in earlier] + [key_vectors], axis=1).reshape(
        batch, window, head_count, DH
    )
    value_window = jnp.concatenate([pair[1] for pair in earlier] + [value_vectors], axis=1).reshape(
        batch, window, head_count, DH
    )
    mask = key_mask(lengths, lax.axis_index("ctx"), rows)
    query_heads = queries.reshape(batch, rows, head_count, DH)
    grad_heads = out_grad.reshape(batch, rows, head_count, DH)
    scores = (
        jnp.einsum("bqhd,bkhd->bhqk", query_heads, key_window, preferred_element_type=jnp.float32)
        * scale
    )
    scores = jnp.where(mask[:, None], scores, -jnp.inf)
    peak = jnp.max(scores, axis=3, keepdims=True)
    totals = jnp.sum(jnp.exp(scores - peak), axis=3, keepdims=True)
    log_totals = peak + jnp.log(totals)
    weights = jnp.exp(scores - log_totals)
    weights_low = weights.astype(jnp.bfloat16)
    attended = jnp.einsum(
        "bhqk,bkhd->bqhd", weights_low, value_window, preferred_element_type=jnp.float32
    ).astype(jnp.bfloat16)
    along = jnp.sum(attended.astype(jnp.float32) * grad_heads.astype(jnp.float32), axis=3)
    along = jnp.transpose(along, (0, 2, 1))[..., None]
    pulls = jnp.einsum(
        "bqhd,bkhd->bhqk", grad_heads, value_window, preferred_element_type=jnp.float32
    )
    slopes = (weights * (pulls - along)).astype(jnp.bfloat16)
    query_grad = (
        jnp.einsum("bhqk,bkhd->bqhd", slopes, key_window, preferred_element_type=jnp.float32)
        * scale
    ).astype(jnp.bfloat16)
    key_terms = (
        jnp.einsum("bhqk,bqhd->bkhd", slopes, query_heads, preferred_element_type=jnp.float32)
        * scale
    )
    key_terms = key_terms.reshape(batch, SPAN + 1, rows, width)
    value_terms = jnp.einsum(
        "bhqk,bqhd->bkhd", weights_low, grad_heads, preferred_element_type=jnp.float32
    )
    value_terms = value_terms.reshape(batch, SPAN + 1, rows, width)
    key_total = key_terms[:, SPAN]
    value_total = value_terms[:, SPAN]
    for offset in range(SPAN):
        returned = from_behind(
            (
                key_terms[:, offset].astype(jnp.bfloat16),
                value_terms[:, offset].astype(jnp.bfloat16),
            ),
            "ctx",
            offset - SPAN,
        )
        key_total = key_total + returned[0].astype(jnp.float32)
        value_total = value_total + returned[1].astype(jnp.float32)
    return (
        attended.reshape(batch, rows, width),
        log_totals[..., 0],
        query_grad.reshape(batch, rows, width),
        key_total.astype(jnp.bfloat16),
        value_total.astype(jnp.bfloat16),
    )


def shards(queries, key_vectors, value_vectors, out_grad, doc_lengths):
    results = attend(queries, key_vectors, value_vectors, out_grad, doc_lengths)
    return results


def solution(mesh):
    in_specs = (
        P("dp", "ctx", None),
        P("dp", "ctx", None),
        P("dp", "ctx", None),
        P("dp", "ctx", None),
        P("dp", None),
    )
    out_specs = (
        P("dp", "ctx", None),
        P("dp", None, "ctx"),
        P("dp", "ctx", None),
        P("dp", "ctx", None),
        P("dp", "ctx", None),
    )
    return jax.shard_map(shards, mesh=mesh, in_specs=in_specs, out_specs=out_specs, check_vma=False)
```

profile of v0, /device:TPU:32, one launch (start us, length us, event | category | flops | bytes accessed | tf_op | source)
XLA Modules:
  0.0 1032.4 jit_solution(9432822418869998909)
XLA Ops:
  25.7 29.4 %collective-permute-done.1 = bf16[1,128,8192]{2,1,0:T(8,128)(2,1)S(1)} collective-permute-done((bf16[1,128,8192]{2,1,0:T(8,128)(2,1)}, bf16[1,128,8192]{2,1,0:T(8,128)(2,1)S(1)}, u32[]{:S(2)}, u32[]{:S(2)}) %collective-permute-start.1) | collective-permute-done | bytes 2097184 | tf_op jit(solution)/shard_map/ppermute | solution.py:13
  68.0 96.7 %collective-permute-done = bf16[1,128,8192]{2,1,0:T(8,128)(2,1)} collective-permute-done((bf16[1,128,8192]{2,1,0:T(8,128)(2,1)}, bf16[1,128,8192]{2,1,0:T(8,128)(2,1)}, u32[]{:S(2)}, u32[]{:S(2)}) %collective-permute-start) | collective-permute-done | bytes 2097184 | tf_op jit(solution)/shard_map/ppermute | solution.py:13
  171.7 12.0 %copy.114 = bf16[1,512,8192]{1,2,0:T(8,128)(2,1)} copy(bf16[1,512,8192]{2,1,0:T(8,128)(2,1)} %pad_maximum_fusion) | data formatting | bytes 16777216 | tf_op jit(solution)/shard_map/concatenate | solution.py:38
  183.7 66.1 %collective-permute-done.5 = bf16[1,128,8192]{1,2,0:T(8,128)(2,1)} collective-permute-done((bf16[1,128,8192]{1,2,0:T(8,128)(2,1)}, bf16[1,128,8192]{1,2,0:T(8,128)(2,1)}, u32[]{:S(2)}, u32[]{:S(2)}) %collective-permute-start.5) | collective-permute-done | bytes 2097184 | tf_op jit(solution)/shard_map/ppermute | solution.py:13
  249.8 27.5 %collective-permute-done.3 = bf16[1,128,8192]{1,2,0:T(8,128)(2,1)} collective-permute-done((bf16[1,128,8192]{1,2,0:T(8,128)(2,1)}, bf16[1,128,8192]{1,2,0:T(8,128)(2,1)}, u32[]{:S(2)}, u32[]{:S(2)}) %collective-permute-start.3) | collective-permute-done | bytes 2097184 | tf_op jit(solution)/shard_map/ppermute | solution.py:13
  284.4 14.1 %fusion.2 = (f32[64,128]{1,0:T(8,128)S(1)}, f32[64,512,128]{2,1,0:T(8,128)}) fusion(pred[128,512]{0,1:T(8,128)(4,1)S(1)} %compare_and_fusion, bf16[512,64,128]{0,2,1:T(8,128)(2,1)} %bitcast.98, bf16[128,64,128]{2,1,0:T(8,128)(2,1)S(1)} %bitcast.106), kind=kOutput, calls=%fused_computation.7 | convolution fusion | flops 1086316544 | bytes 27361280 | tf_op jit(solution)/shard_map/bqhd,bkhd->bhqk/dot_general | solution.py:45
  307.9 12.9 %convolution_bitcast_fusion = f32[1,512,64,128]{3,1,2,0:T(8,128)} fusion(bf16[128,64,128]{2,1,0:T(8,128)(2,1)} %bitcast.110, f32[64,512,128]{2,1,0:T(8,128)} %get-tuple-element.42, f32[64,128]{1,0:T(8,128)S(1)} %log_add_fusion, pred[128,512]{0,1:T(8,128)(4,1)S(1)} %compare_and_fusion), kind=kOutput, calls=%fused_computation.8 | convolution fusion | flops 1090519040 | bytes 35749888 | tf_op jit(solution)/shard_map/bhqk,bqhd->bkhd/dot_general | solution.py:72
  320.8 16.4 %multiply_reduce_fusion = (f32[128,64]{0,1:T(8,128)S(1)}, bf16[64,128,128]{2,1,0:T(8,128)(2,1)}) fusion(f32[1,128,64,128]{1,3,2,0:T(8,128)} %bitcast.114, bf16[512,64,128]{0,2,1:T(8,128)(2,1)} %bitcast.112, f32[64,512,128]{2,1,0:T(8,128)} %get-tuple-element.42, f32[64,128]{1,0:T(8,128)S(1)} %log_add_fusion, pred[128,512]{0,1:T(8,128)(4,1)S(1)} %compare_and_fusion), kind=kOutput, calls=%fused_computation.26 | convolution fusion | flops 1094705152 | bytes 31588352 | tf_op jit(solution)/shard_map/bhqk,bkhd->bqhd/dot_general | solution.py:54
  337.2 15.4 %fusion = bf16[64,128,512]{1,2,0:T(8,128)(2,1)} fusion(f32[64,512,128]{2,1,0:T(8,128)} %get-tuple-element.42, bf16[512,64,128]{0,2,1:T(8,128)(2,1)} %bitcast.113, f32[64,128]{1,0:T(8,128)S(1)} %bitcast.118, f32[64,128]{1,0:T(8,128)S(1)} %log_add_fusion, pred[128,512]{0,1:T(8,128)(4,1)S(1)} %compare_and_fusion, bf16[128,64,128]{2,1,0:T(8,128)(2,1)} %bitcast.111), kind=kOutput, calls=%fused_computation.1 | convolution fusion | flops 1098907648 | bytes 35782656 | tf_op jit(solution)/shard_map/bqhd,bkhd->bhqk/dot_general | solution.py:59
  352.6 9.6 multiply_convert_fusion
  370.6 17.8 %copy.132 = f32[1,512,64,128]{3,2,0,1:T(8,128)} copy(f32[1,512,64,128]{3,1,2,0:T(8,128)} %convolution_bitcast_fusion) | data formatting | bytes 33554432 | tf_op jit(solution)/shard_map/bhqk,bqhd->bkhd/transpose | solution.py:72
  395.4 15.6 %copy.127 = f32[1,512,64,128]{3,2,0,1:T(8,128)S(1)} copy(f32[1,512,64,128]{3,1,2,0:T(8,128)} %multiply_bitcast_fusion) | data formatting | bytes 33554432 | tf_op jit(solution)/shard_map/mul | solution.py:68
  416.8 15.1 %convert.11 = bf16[1,4,128,8192]{3,0,2,1:T(2,128)(2,1)} convert(f32[1,4,128,8192]{3,0,2,1:T(1,128)S(1)} %bitcast.104) | non-fusion elementwise | flops 4194304 | bytes 25165824 | tf_op jit(solution)/shard_map/convert.6
  431.9 20.4 %slice_bitcast_fusion.6 = (bf16[1,128,8192]{2,0,1:T(2,128)(2,1)}, bf16[1,128,8192]{2,0,1:T(2,128)(2,1)}, bf16[1,128,8192]{2,0,1:T(2,128)(2,1)}) fusion(bf16[1,4,128,8192]{3,0,2,1:T(2,128)(2,1)} %convert.11), kind=kLoop, calls=%fused_computation.20 | loop fusion | bytes 12582912 | tf_op jit(solution)/shard_map/convert_element_type | solution.py:81
  459.0 15.2 %convert.12 = bf16[1,4,128,8192]{3,0,2,1:T(2,128)(2,1)} convert(f32[1,4,128,8192]{3,0,2,1:T(1,128)S(1)} %bitcast.102) | non-fusion elementwise | flops 4194304 | bytes 25165824 | tf_op jit(solution)/shard_map/convert.3
  474.2 20.2 %slice_bitcast_fusion.2 = (bf16[1,128,8192]{2,0,1:T(2,128)(2,1)}, bf16[1,128,8192]{2,0,1:T(2,128)(2,1)}, bf16[1,128,8192]{2,0,1:T(2,128)(2,1)}) fusion(bf16[1,4,128,8192]{3,0,2,1:T(2,128)(2,1)} %convert.12), kind=kLoop, calls=%fused_computation.13 | loop fusion | bytes 12582912 | tf_op jit(solution)/shard_map/convert_element_type | solution.py:82
  498.9 50.3 %collective-permute-done.6 = bf16[1,128,8192]{2,0,1:T(2,128)(2,1)S(1)} collective-permute-done((bf16[1,128,8192]{2,0,1:T(2,128)(2,1)}, bf16[1,128,8192]{2,0,1:T(2,128)(2,1)S(1)}, u32[]{:S(2)}, u32[]{:S(2)}) %collective-permute-start.6) | collective-permute-done | bytes 2097184 | tf_op jit(solution)/shard_map/ppermute | solution.py:13
  549.1 89.9 %collective-permute-start.10 = (bf16[1,128,8192]{2,0,1:T(2,128)(2,1)}, bf16[1,128,8192]{2,0,1:T(2,128)(2,1)}, u32[]{:S(2)}, u32[]{:S(2)}) collective-permute-start(bf16[1,128,8192]{2,0,1:T(2,128)(2,1)} %get-tuple-element.37), channel_id=1, source_target_pairs={{2,0},{3,1},{4,2},{5,3},{6,4},{7,5},{8,6},{9,7},{10,8},{11,9},{12,... | collective-permute-start | bytes 6291464 | tf_op jit(solution)/shard_map/ppermute | solution.py:13
  639.0 57.8 %collective-permute-done.8 = bf16[1,128,8192]{2,0,1:T(2,128)(2,1)S(1)} collective-permute-done((bf16[1,128,8192]{2,0,1:T(2,128)(2,1)}, bf16[1,128,8192]{2,0,1:T(2,128)(2,1)S(1)}, u32[]{:S(2)}, u32[]{:S(2)}) %collective-permute-start.8) | collective-permute-done | bytes 2097184 | tf_op jit(solution)/shard_map/ppermute | solution.py:13
  696.8 12.9 %fusion.9 = bf16[1,128,8192]{2,0,1:T(2,128)(2,1)S(1)} fusion(bf16[1,128,8192]{2,0,1:T(2,128)(2,1)S(1)} %collective-permute-done.8, bf16[1,128,8192]{2,0,1:T(2,128)(2,1)} %collective-permute-done.7, bf16[1,128,8192]{2,0,1:T(2,128)(2,1)S(1)} %collective-permute-done.6, f32[1,4,128,8192]{3,0,2,1:T(1,128)} %bitcast.105), kind=kLoop, calls=%fused_computation.27 | loop fusion | flops 7340032 | bytes 12582912 | tf_op jit(solution)/shard_map/convert_element_type | solution.py:93
  713.4 13.4 %collective-permute-done.9 = bf16[1,128,8192]{2,0,1:T(2,128)(2,1)S(1)} collective-permute-done((bf16[1,128,8192]{2,0,1:T(2,128)(2,1)}, bf16[1,128,8192]{2,0,1:T(2,128)(2,1)S(1)}, u32[]{:S(2)}, u32[]{:S(2)}) %collective-permute-start.9) | collective-permute-done | bytes 2097184 | tf_op jit(solution)/shard_map/ppermute | solution.py:13
  726.8 236.4 %collective-permute-done.11 = bf16[1,128,8192]{2,0,1:T(2,128)(2,1)S(1)} collective-permute-done((bf16[1,128,8192]{2,0,1:T(2,128)(2,1)}, bf16[1,128,8192]{2,0,1:T(2,128)(2,1)S(1)}, u32[]{:S(2)}, u32[]{:S(2)}) %collective-permute-start.11) | collective-permute-done | bytes 2097184 | tf_op jit(solution)/shard_map/ppermute | solution.py:13
  963.2 52.8 %collective-permute-done.10 = bf16[1,128,8192]{2,0,1:T(2,128)(2,1)} collective-permute-done((bf16[1,128,8192]{2,0,1:T(2,128)(2,1)}, bf16[1,128,8192]{2,0,1:T(2,128)(2,1)}, u32[]{:S(2)}, u32[]{:S(2)}) %collective-permute-start.10) | collective-permute-done | bytes 2097184 | tf_op jit(solution)/shard_map/ppermute | solution.py:13
  1016.0 12.6 %fusion.10 = bf16[1,128,8192]{2,0,1:T(2,128)(2,1)S(1)} fusion(bf16[1,128,8192]{2,0,1:T(2,128)(2,1)S(1)} %collective-permute-done.11, bf16[1,128,8192]{2,0,1:T(2,128)(2,1)} %collective-permute-done.10, bf16[1,128,8192]{2,0,1:T(2,128)(2,1)S(1)} %collective-permute-done.9, f32[1,4,128,8192]{3,0,2,1:T(1,128)S(1)} %bitcast.103), kind=kLoop, calls=%fused_computation.28 | loop fusion | flops 7340032 | bytes 12582912 | tf_op jit(solution)/shard_map/convert_element_type | solution.py:94
  (54 shorter events, 100.8 us)
Async XLA Ops:
  0.6 54.5 %collective-permute-start.1 = (bf16[1,128,8192]{2,1,0:T(8,128)(2,1)}, bf16[1,128,8192]{2,1,0:T(8,128)(2,1)S(1)}, u32[]{:S(2)}, u32[]{:S(2)}) collective-permute-start(bf16[1,128,8192]{2,1,0:T(8,128)(2,1)} %param.7), channel_id=1, source_target_pairs={{0,2},{1,3},{2,4},{3,5},{4,6},{5,7},{6,8},{7,9},{8,10},{9,11},{10,... | collective-permute-start | bytes 6291464 | tf_op jit(solution)/shard_map/ppermute | solution.py:13
  5.6 159.1 %collective-permute-start = (bf16[1,128,8192]{2,1,0:T(8,128)(2,1)}, bf16[1,128,8192]{2,1,0:T(8,128)(2,1)}, u32[]{:S(2)}, u32[]{:S(2)}) collective-permute-start(bf16[1,128,8192]{2,1,0:T(8,128)(2,1)} %param.7), channel_id=1, source_target_pairs={{0,3},{1,4},{2,5},{3,6},{4,7},{5,8},{6,9},{7,10},{8,11},{9,12},{10... | collective-permute-start | bytes 6291464 | tf_op jit(solution)/shard_map/ppermute | solution.py:13
  10.0 154.7 %collective-permute-start.2 = (bf16[1,128,8192]{2,1,0:T(8,128)(2,1)}, bf16[1,128,8192]{2,1,0:T(8,128)(2,1)}, u32[]{:S(2)}, u32[]{:S(2)}) collective-permute-start(bf16[1,128,8192]{2,1,0:T(8,128)(2,1)} %param.7), channel_id=1, source_target_pairs={{0,1},{1,2},{2,3},{3,4},{4,5},{5,6},{6,7},{7,8},{8,9},{9,10},{10,1... | collective-permute-start | bytes 6291464 | tf_op jit(solution)/shard_map/ppermute | solution.py:13
  16.9 50.7 %copy-start.5 = (s32[1,16]{1,0:T(1,128)S(1)}, s32[1,16]{1,0:T(1,128)}, u32[]{:S(2)}) copy-start(s32[1,16]{1,0:T(1,128)} %param.9) | copy-start | bytes 196
  16.9 232.9 %collective-permute-start.5 = (bf16[1,128,8192]{1,2,0:T(8,128)(2,1)}, bf16[1,128,8192]{1,2,0:T(8,128)(2,1)}, u32[]{:S(2)}, u32[]{:S(2)}) collective-permute-start(bf16[1,128,8192]{1,2,0:T(8,128)(2,1)} %copy.115), channel_id=1, source_target_pairs={{0,1},{1,2},{2,3},{3,4},{4,5},{5,6},{6,7},{7,8},{8,9},{9,10},{10,1... | collective-permute-start | bytes 6291464 | tf_op jit(solution)/shard_map/ppermute | solution.py:13
  19.5 230.3 %collective-permute-start.4 = (bf16[1,128,8192]{1,2,0:T(8,128)(2,1)}, bf16[1,128,8192]{1,2,0:T(8,128)(2,1)}, u32[]{:S(2)}, u32[]{:S(2)}) collective-permute-start(bf16[1,128,8192]{1,2,0:T(8,128)(2,1)} %copy.115), channel_id=1, source_target_pairs={{0,2},{1,3},{2,4},{3,5},{4,6},{5,7},{6,8},{7,9},{8,10},{9,11},{10,... | collective-permute-start | bytes 6291464 | tf_op jit(solution)/shard_map/ppermute | solution.py:13
  55.1 2.3 copy-start.3
  55.1 222.2 %collective-permute-start.3 = (bf16[1,128,8192]{1,2,0:T(8,128)(2,1)}, bf16[1,128,8192]{1,2,0:T(8,128)(2,1)}, u32[]{:S(2)}, u32[]{:S(2)}) collective-permute-start(bf16[1,128,8192]{1,2,0:T(8,128)(2,1)} %copy.115), channel_id=1, source_target_pairs={{0,3},{1,4},{2,5},{3,6},{4,7},{5,8},{6,9},{7,10},{8,11},{9,12},{10... | collective-permute-start | bytes 6291464 | tf_op jit(solution)/shard_map/ppermute | solution.py:13
  307.9 29.3 %copy-start.4 = (f32[64,128]{1,0:T(8,128)}, f32[64,128]{1,0:T(8,128)S(1)}, u32[]{:S(2)}) copy-start(f32[64,128]{1,0:T(8,128)S(1)} %log_add_fusion) | copy-start | bytes 98308
  352.6 9.6 copy-start.1
  370.6 17.9 %copy-start.2 = (bf16[64,128,128]{2,1,0:T(8,128)(2,1)S(1)}, bf16[64,128,128]{2,1,0:T(8,128)(2,1)}, u32[]{:S(2)}) copy-start(bf16[64,128,128]{2,1,0:T(8,128)(2,1)} %multiply_convert_fusion) | copy-start | bytes 6291460
  411.0 5.7 copy-start
  416.8 42.2 %slice-start = ((s8[16777216]{0:T(1024)(128)(4,1)}), s8[4194304]{0:T(1024)(128)(4,1)S(1)}, s32[]{:S(2)}) async-start(s8[16777216]{0:T(1024)(128)(4,1)} %bitcast.100), calls=%async_computation | async-start | bytes 8388608
  416.8 42.2 %slice-start.1 = ((s8[16777216]{0:T(1024)(128)(4,1)}), s8[4194304]{0:T(1024)(128)(4,1)S(1)}, s32[]{:S(2)}) async-start(s8[16777216]{0:T(1024)(128)(4,1)} %bitcast.100), calls=%async_computation.1 | async-start | bytes 8388608
  416.8 42.2 %slice-start.2 = ((s8[16777216]{0:T(1024)(128)(4,1)}), s8[4194304]{0:T(1024)(128)(4,1)S(1)}, s32[]{:S(2)}) async-start(s8[16777216]{0:T(1024)(128)(4,1)} %bitcast.100), calls=%async_computation.2 | async-start | bytes 8388608
  431.9 27.1 %slice-start.3 = ((s8[16777216]{0:T(1024)(128)(4,1)}), s8[4194304]{0:T(1024)(128)(4,1)S(1)}, s32[]{:S(2)}) async-start(s8[16777216]{0:T(1024)(128)(4,1)} %bitcast.100), calls=%async_computation.3 | async-start | bytes 8388608
  452.3 96.8 %collective-permute-start.6 = (bf16[1,128,8192]{2,0,1:T(2,128)(2,1)}, bf16[1,128,8192]{2,0,1:T(2,128)(2,1)S(1)}, u32[]{:S(2)}, u32[]{:S(2)}) collective-permute-start(bf16[1,128,8192]{2,0,1:T(2,128)(2,1)} %get-tuple-element.38), channel_id=1, source_target_pairs={{3,0},{4,1},{5,2},{6,3},{7,4},{8,5},{9,6},{10,7},{11,8},{12,9},{13... | collective-permute-start | bytes 6291464 | tf_op jit(solution)/shard_map/ppermute | solution.py:13
  454.2 242.6 %collective-permute-start.8 = (bf16[1,128,8192]{2,0,1:T(2,128)(2,1)}, bf16[1,128,8192]{2,0,1:T(2,128)(2,1)S(1)}, u32[]{:S(2)}, u32[]{:S(2)}) collective-permute-start(bf16[1,128,8192]{2,0,1:T(2,128)(2,1)} %get-tuple-element.39), channel_id=1, source_target_pairs={{1,0},{2,1},{3,2},{4,3},{5,4},{6,5},{7,6},{8,7},{9,8},{10,9},{11,1... | collective-permute-start | bytes 6291464 | tf_op jit(solution)/shard_map/ppermute | solution.py:13
  456.1 240.7 %collective-permute-start.7 = (bf16[1,128,8192]{2,0,1:T(2,128)(2,1)}, bf16[1,128,8192]{2,0,1:T(2,128)(2,1)}, u32[]{:S(2)}, u32[]{:S(2)}) collective-permute-start(bf16[1,128,8192]{2,0,1:T(2,128)(2,1)} %get-tuple-element.40), channel_id=1, source_target_pairs={{2,0},{3,1},{4,2},{5,3},{6,4},{7,5},{8,6},{9,7},{10,8},{11,9},{12,... | collective-permute-start | bytes 6291464 | tf_op jit(solution)/shard_map/ppermute | solution.py:13
  494.4 232.3 %collective-permute-start.9 = (bf16[1,128,8192]{2,0,1:T(2,128)(2,1)}, bf16[1,128,8192]{2,0,1:T(2,128)(2,1)S(1)}, u32[]{:S(2)}, u32[]{:S(2)}) collective-permute-start(bf16[1,128,8192]{2,0,1:T(2,128)(2,1)} %get-tuple-element.35), channel_id=1, source_target_pairs={{3,0},{4,1},{5,2},{6,3},{7,4},{8,5},{9,6},{10,7},{11,8},{12,9},{13... | collective-permute-start | bytes 6291464 | tf_op jit(solution)/shard_map/ppermute | solution.py:13
  496.3 466.8 %collective-permute-start.11 = (bf16[1,128,8192]{2,0,1:T(2,128)(2,1)}, bf16[1,128,8192]{2,0,1:T(2,128)(2,1)S(1)}, u32[]{:S(2)}, u32[]{:S(2)}) collective-permute-start(bf16[1,128,8192]{2,0,1:T(2,128)(2,1)} %get-tuple-element.36), channel_id=1, source_target_pairs={{1,0},{2,1},{3,2},{4,3},{5,4},{6,5},{7,6},{8,7},{9,8},{10,9},{11,1... | collective-permute-start | bytes 6291464 | tf_op jit(solution)/shard_map/ppermute | solution.py:13
  549.1 466.9 %collective-permute-start.10 = (bf16[1,128,8192]{2,0,1:T(2,128)(2,1)}, bf16[1,128,8192]{2,0,1:T(2,128)(2,1)}, u32[]{:S(2)}, u32[]{:S(2)}) collective-permute-start(bf16[1,128,8192]{2,0,1:T(2,128)(2,1)} %get-tuple-element.37), channel_id=1, source_target_pairs={{2,0},{3,1},{4,2},{5,3},{6,4},{7,5},{8,6},{9,7},{10,8},{11,9},{12,... | collective-permute-start | bytes 6291464 | tf_op jit(solution)/shard_map/ppermute | solution.py:13
where the time goes:
time: 1040 us; the launch traced here: 1030 us
  waiting for transfers between devices  630 us (61%)
  starting transfers between devices  124 us (12%)
  local copies, waits for them, and re-layouts  120 us (12%)
  other arithmetic  79.7 us (8%)
  matrix products  76.8 us (7%)
    ppermute x12, waiting for transfers between devices, from_behind(): return lax.ppermute(block, axis, route)  630 us
    ppermute x12, starting transfers between devices, from_behind(): return lax.ppermute(block, axis, route)  124 us
    another operation x2, other arithmetic  30.3 us
    unnamed x27, local copies, waits for them, and re-layouts  29.7 us
  transfers between devices with their start and end apart: 12, of which 9 were waited for; matrix products, arithmetic and copies ran while one was open for 8% of the time, Pallas kernels for 0%

commit v1 on v0

v1 whole, which is shorter than its diff:
```python
import functools

import jax
import jax.numpy as jnp
from jax import lax
from jax.experimental import pallas as pl
from jax.experimental.pallas import tpu as pltpu
from jax.sharding import PartitionSpec as P

DH = 128
SPAN = 3
ROWS = 128
RING = 4
WINDOW = (SPAN + 1) * ROWS
CHUNKS = 4
AHEAD = 2
LOG2E = 1.4426950408889634
LN2 = 0.6931471805599453
MASKED = -1e30
MESH = pl.DeviceIdType.MESH

NT = (((1,), (1,)), ((), ()))
NN = (((1,), (0,)), ((), ()))
TN = (((0,), (0,)), ((), ()))


def dot(a, b, dims):
    return lax.dot_general(a, b, dims, preferred_element_type=jnp.float32)


def kernel(
    group,
    lengths,
    q_in,
    k_in,
    v_in,
    g_in,
    o_out,
    lse_out,
    dq_out,
    dk_out,
    dv_out,
    qb,
    kb,
    vb,
    gb,
    ob,
    dqb,
    lseb,
    own_k,
    own_v,
    far_k,
    far_v,
    near_k,
    near_v,
    fin_k,
    fin_v,
    bias,
    in_send,
    in_recv,
    halo_send,
    halo_recv,
    back_send,
    back_recv,
    out_send,
    out_recv,
    lse_send,
    lse_recv,
    in_local,
    out_local,
    lse_local,
):
    heads = group // DH
    width = group // CHUNKS
    per_chunk = width // DH
    dp = lax.axis_index("dp")
    ctx = lax.axis_index("ctx")
    z, x = ctx // RING, ctx % RING
    rings = lax.axis_size("ctx") // RING
    ahead = (dp, ((z + 1) % rings) * RING + x)
    behind = (dp, ((z + rings - 1) % rings) * RING + x)

    def at(step):
        return (x + step) % RING

    def peer(step):
        return (dp, z * RING + at(step))

    def span(start, size):
        return pl.ds(pl.multiple_of(start, DH), size)

    steps = (2, 1, 3)
    inputs = ((k_in, kb, SPAN), (v_in, vb, SPAN), (q_in, qb, 0), (g_in, gb, 0))

    barrier = pltpu.get_barrier_semaphore()
    for device in (peer(1), peer(2), peer(3), ahead, behind):
        pl.semaphore_signal(barrier, inc=1, device_id=device, device_id_type=MESH)
    pl.semaphore_wait(barrier, 5)

    def input_copy(c, a, step, sender):
        source, buffer, first = inputs[a]
        return pltpu.make_async_remote_copy(
            source.at[0, :, span(at(step) * group + c * width, width)],
            buffer.at[first + sender, :, span(c * width, width)],
            in_send.at[c, a, step - 1],
            in_recv.at[c, a, step - 1],
            device_id=peer(step),
            device_id_type=MESH,
        )

    def send_inputs(c):
        for a in range(4):
            for step in steps:
                input_copy(c, a, step, x).start()

    def wait_inputs(c, arrays):
        for a in arrays:
            for step in steps:
                input_copy(c, a, step, at(RING - step)).wait_recv()

    def local_input(a):
        source, buffer, first = inputs[a]
        return pltpu.make_async_copy(
            source.at[0, :, span(x * group, group)], buffer.at[first + x], in_local.at[a]
        )

    def halo_copy(c, a):
        buffer = (kb, vb)[a]
        columns = span(c * width, width)
        return pltpu.make_async_remote_copy(
            buffer.at[pl.ds(RING, SPAN), :, columns],
            buffer.at[pl.ds(0, SPAN), :, columns],
            halo_send.at[c, a],
            halo_recv.at[c, a],
            device_id=ahead,
            device_id_type=MESH,
        )

    def back_copy(c, a):
        columns = span(c * width, width)
        return pltpu.make_async_remote_copy(
            (far_k, far_v)[a].at[:, :, columns],
            (near_k, near_v)[a].at[:, :, columns],
            back_send.at[c, a],
            back_recv.at[c, a],
            device_id=behind,
            device_id_type=MESH,
        )

    outputs = ((ob, o_out), (dqb, dq_out), (fin_k, dk_out), (fin_v, dv_out))

    def output_copy(c, a, step):
        staged, out = outputs[a]
        return pltpu.make_async_remote_copy(
            staged.at[at(step), :, span(c * width, width)],
            out.at[0, :, span(x * group + c * width, width)],
            out_send.at[c, a, step - 1],
            out_recv.at[c, a, step - 1],
            device_id=peer(step),
            device_id_type=MESH,
        )

    def arrived_output(c, a, step):
        staged, out = outputs[a]
        return pltpu.make_async_remote_copy(
            staged.at[at(step), :, span(c * width, width)],
            out.at[0, :, span(at(RING - step) * group + c * width, width)],
            out_send.at[c, a, step - 1],
            out_recv.at[c, a, step - 1],
            device_id=peer(step),
            device_id_type=MESH,
        )

    def local_output(c, a):
        staged, out = outputs[a]
        return pltpu.make_async_copy(
            staged.at[x, :, span(c * width, width)],
            out.at[0, :, span(x * group + c * width, width)],
            out_local.at[c, a],
        )

    def send_outputs(c, arrays):
        for a in arrays:
            for step in steps:
                output_copy(c, a, step).start()
            local_output(c, a).start()

    def lse_copy(step, sender):
        return pltpu.make_async_remote_copy(
            lseb.at[at(step)],
            lse_out.at[0, pl.ds(pl.multiple_of(sender * heads, 8), heads), :],
            lse_send.at[step - 1],
            lse_recv.at[step - 1],
            device_id=peer(step),
            device_id_type=MESH,
        )

    for c in range(AHEAD):
        send_inputs(c)
    for a in range(4):
        local_input(a).start()

    for i in range(RING):
        base = (z * RING + i) * ROWS
        query_pos = base + lax.broadcasted_iota(jnp.int32, (1, ROWS), 1)
        first = jnp.zeros((1, ROWS), jnp.int32)
        start = jnp.int32(0)
        for d in range(lengths.shape[1]):
            first = jnp.where(start <= query_pos, start, first)
            start = start + lengths[0, d]
        key_pos = base - SPAN * ROWS + lax.broadcasted_iota(jnp.int32, (WINDOW, ROWS), 0)
        bias[i] = jnp.where((key_pos >= first) & (key_pos <= query_pos), 0.0, MASKED)

    for a in range(4):
        local_input(a).wait()

    scale = DH ** (-0.5)

    def one_head(h):
        columns = span(h * DH, DH)
        weights, slopes, query_blocks, grad_blocks = [], [], [], []
        for i in range(RING):
            keys = kb[i : i + SPAN + 1, :, columns].reshape(WINDOW, DH)
            values = vb[i : i + SPAN + 1, :, columns].reshape(WINDOW, DH)
            queries = qb[i, :, columns]
            grads = gb[i, :, columns]
            scores = dot(keys, queries, NT) * (scale * LOG2E) + bias[i]
            peak = jnp.max(scores, axis=0, keepdims=True)
            powers = jnp.exp2(scores - peak)
            totals = jnp.sum(powers, axis=0, keepdims=True)
            lseb[i, pl.ds(h, 1), :] = (peak + jnp.log2(totals)) * LN2
            weight = powers * (1.0 / totals)
            weight_low = weight.astype(jnp.bfloat16)
            pulls = dot(values, grads, NT)
            weighted = weight * pulls
            along = jnp.sum(weighted, axis=0, keepdims=True)
            slope = (weighted - weight * along).astype(jnp.bfloat16)
            ob[i, :, columns] = dot(weight_low, values, TN).astype(jnp.bfloat16)
            dqb[i, :, columns] = (dot(slope, keys, TN) * scale).astype(jnp.bfloat16)
            weights.append(weight_low)
            slopes.append(slope)
            query_blocks.append(queries)
            grad_blocks.append(grads)
        for j in range(SPAN + RING):
            seen = range(max(0, j - SPAN), min(RING - 1, j) + 1)

            def gather(parts):
                return jnp.concatenate(
                    [parts[i][(j - i) * ROWS : (j - i + 1) * ROWS] for i in seen], axis=1
                )

            def stack(blocks):
                return jnp.concatenate([blocks[i] for i in seen], axis=0)

            key_part = dot(gather(slopes), stack(query_blocks), NN) * scale
            value_part = dot(gather(weights), stack(grad_blocks), NN)
            if j < SPAN:
                far_k[j, :, columns] = key_part.astype(jnp.bfloat16)
                far_v[j, :, columns] = value_part.astype(jnp.bfloat16)
            else:
                own_k[j - SPAN, :, columns] = key_part
                own_v[j - SPAN, :, columns] = value_part

    def finish(c):
        columns = span(c * width, width)
        for a, (own, near, fin) in enumerate(
            ((own_k, near_k, fin_k), (own_v, near_v, fin_v))
        ):
            back_copy(c, a).wait_recv()
            fin[0, :, columns] = own[0, :, columns].astype(jnp.bfloat16)
            for s in range(1, RING):
                total = own[s, :, columns] + near[s - 1, :, columns].astype(jnp.float32)
                fin[s, :, columns] = total.astype(jnp.bfloat16)
        send_outputs(c, (2, 3))

    def one_chunk(c, carry):
        wait_inputs(c, (0, 1))
        for a in range(2):
            halo_copy(c, a).start()

        @pl.when(c + AHEAD < CHUNKS)
        def _():
            send_inputs(c + AHEAD)

        wait_inputs(c, (2, 3))
        for a in range(2):
            halo_copy(c, a).wait_recv()

        def head_step(h, inner):
            one_head(c * per_chunk + h)
            return inner

        lax.fori_loop(0, per_chunk, head_step, 0)
        for a in range(2):
            back_copy(c, a).start()
        send_outputs(c, (0, 1))

        @pl.when(c >= 1)
        def _():
            finish(c - 1)

        return carry

    lax.fori_loop(0, CHUNKS, one_chunk, 0)
    for step in steps:
        lse_copy(step, x).start()
    own_lse = pltpu.make_async_copy(
        lseb.at[x], lse_out.at[0, pl.ds(pl.multiple_of(x * heads, 8), heads), :], lse_local.at[0]
    )
    own_lse.start()
    finish(CHUNKS - 1)

    def drain(c, carry):
        for a in range(2):
            halo_copy(c, a).wait_send()
            back_copy(c, a).wait_send()
        for a in range(4):
            local_output(c, a).wait()
            for step in steps:
                input_copy(c, a, step, x).wait_send()
                output_copy(c, a, step).wait_send()
                arrived_output(c, a, step).wait_recv()
        return carry

    lax.fori_loop(0, CHUNKS, drain, 0)
    own_lse.wait()
    for step in steps:
        lse_copy(step, x).wait_send()
        lse_copy(step, at(RING - step)).wait_recv()


def attend(queries, key_vectors, value_vectors, out_grad, lengths):
    _, rows, all_width = queries.shape
    group = all_width // RING
    heads = group // DH
    block = jax.ShapeDtypeStruct(queries.shape, jnp.bfloat16)
    totals = jax.ShapeDtypeStruct((1, all_width // DH, rows), jnp.float32)
    anywhere = pl.BlockSpec(memory_space=pl.ANY)
    low = functools.partial(pltpu.VMEM, dtype=jnp.bfloat16)
    wide = functools.partial(pltpu.VMEM, dtype=jnp.float32)
    copies = pltpu.SemaphoreType.DMA
    return pl.pallas_call(
        functools.partial(kernel, group),
        name="spread_heads_attention",
        out_shape=(block, totals, block, block, block),
        in_specs=[pl.BlockSpec(memory_space=pltpu.SMEM)] + [anywhere] * 4,
        out_specs=(anywhere,) * 5,
        scratch_shapes=[
            low((RING, rows, group)),
            low((SPAN + RING, rows, group)),
            low((SPAN + RING, rows, group)),
            low((RING, rows, group)),
            low((RING, rows, group)),
            low((RING, rows, group)),
            wide((RING, heads, rows)),
            wide((RING, rows, group)),
            wide((RING, rows, group)),
            low((SPAN, rows, group)),
            low((SPAN, rows, group)),
            low((SPAN, rows, group)),
            low((SPAN, rows, group)),
            low((RING, rows, group)),
            low((RING, rows, group)),
            wide((RING, WINDOW, ROWS)),
            copies((CHUNKS, 4, 3)),
            copies((CHUNKS, 4, 3)),
            copies((CHUNKS, 2)),
            copies((CHUNKS, 2)),
            copies((CHUNKS, 2)),
            copies((CHUNKS, 2)),
            copies((CHUNKS, 4, 3)),
            copies((CHUNKS, 4, 3)),
            copies((3,)),
            copies((3,)),
            copies((4,)),
            copies((CHUNKS, 4)),
            copies((1,)),
        ],
        compiler_params=pltpu.CompilerParams(
            collective_id=0, has_side_effects=True, vmem_limit_bytes=56 * 2**20
        ),
    )(lengths, queries, key_vectors, value_vectors, out_grad)


def solution(mesh):
    block = P("dp", "ctx", None)
    in_specs = (block, block, block, block, P("dp", None))
    out_specs = (block, P("dp", None, "ctx"), block, block, block)
    return jax.shard_map(attend, mesh=mesh, in_specs=in_specs, out_specs=out_specs, check_vma=False)
```

time: 1040 us -> 202 us (0.19)
  the two profiles are of different devices: /device:TPU:32 before, /device:TPU:1 now
where the time goes in v1:
time: 202 us
  Pallas kernels  191 us (95%)
  local copies, waits for them, and re-layouts  9.88 us (5%)
    pallas_call x1, Pallas kernels, attend(): pl.pallas_call(functools.partial(kernel, group), name='spread_heads_atten...  191 us
    unnamed x13, local copies, waits for them, and re-layouts  9.88 us

profile of v1, /device:TPU:1, one launch (start us, length us, event | category | flops | bytes accessed | tf_op | source)
XLA Modules:
  0.0 202.0 jit_solution(7166412609055747973)
XLA Ops:
  0.6 191.4 %spread_heads_attention.1 = (bf16[1,128,8192]{2,1,0:T(8,128)(2,1)}, f32[1,64,128]{2,1,0:T(8,128)}, bf16[1,128,8192]{2,1,0:T(8,128)(2,1)}, bf16[1,128,8192]{2,1,0:T(8,128)(2,1)}, bf16[1,128,8192]{2,1,0:T(8,128)(2,1)}) custom-call(s32[1,16]{1,0:T(1,128)} %lengths.1, bf16[1,128,8192]{2,1,0:T(8,128)(2,1)} %q_in.1, bf16[1,128,8192]{2,1,0:T(8,128)(2,1)} %k_in.1, ...), custom_call_target="tpu_custom_call" | custom-call | tf_op jit(solution)/shard_map/spread_heads_attention/pallas_call | solution.py:342
  192.1 0.0 copy-start.3
  192.1 0.0 copy-start.2
  192.1 3.2 %copy.15 = bf16[1,128,8192]{2,1,0:T(8,128)(2,1)} copy(bf16[1,128,8192]{2,1,0:T(8,128)(2,1)} %get-tuple-element.10) | data formatting | bytes 4194304
  195.3 0.0 copy-done.3
  195.3 0.6 copy.16
  195.9 0.0 copy-done.2
  195.9 0.0 copy-start.1
  195.9 1.3 copy.17
  197.3 1.0 copy-done.1
  198.3 0.0 copy-start
  198.3 1.3 copy.18
  199.6 1.0 copy-done
  200.6 1.3 copy.19
Async XLA Ops:
  192.1 3.3 %copy-start.3 = (f32[1,64,128]{2,1,0:T(8,128)S(1)}, f32[1,64,128]{2,1,0:T(8,128)}, u32[]{:S(2)}) copy-start(f32[1,64,128]{2,1,0:T(8,128)} %get-tuple-element.11) | copy-start | bytes 98308
  192.1 3.9 %copy-start.2 = (bf16[1,128,8192]{2,1,0:T(8,128)(2,1)S(1)}, bf16[1,128,8192]{2,1,0:T(8,128)(2,1)}, u32[]{:S(2)}) copy-start(bf16[1,128,8192]{2,1,0:T(8,128)(2,1)} %get-tuple-element.12) | copy-start | bytes 6291460
  195.9 2.3 %copy-start.1 = (bf16[1,128,8192]{2,1,0:T(8,128)(2,1)S(1)}, bf16[1,128,8192]{2,1,0:T(8,128)(2,1)}, u32[]{:S(2)}) copy-start(bf16[1,128,8192]{2,1,0:T(8,128)(2,1)} %get-tuple-element.13) | copy-start | bytes 6291460
  198.3 2.3 %copy-start = (bf16[1,128,8192]{2,1,0:T(8,128)(2,1)S(1)}, bf16[1,128,8192]{2,1,0:T(8,128)(2,1)}, u32[]{:S(2)}) copy-start(bf16[1,128,8192]{2,1,0:T(8,128)(2,1)} %get-tuple-element.14) | copy-start | bytes 6291460

commit v2 on v1

--- a/solution.py
+++ b/solution.py
@@ -329,22 +329,31 @@
         lse_copy(step, at(RING - step)).wait_recv()
 
 
+def write_out(*refs):
+    sems = refs[10]
+    moves = [pltpu.make_async_copy(refs[i], refs[5 + i], sems.at[i]) for i in range(5)]
+    for move in moves:
+        move.start()
+    for move in moves:
+        move.wait()
+
+
 def attend(queries, key_vectors, value_vectors, out_grad, lengths):
     _, rows, all_width = queries.shape
     group = all_width // RING
     heads = group // DH
-    block = jax.ShapeDtypeStruct(queries.shape, jnp.bfloat16)
-    totals = jax.ShapeDtypeStruct((1, all_width // DH, rows), jnp.float32)
+    block = pltpu.VMEM(queries.shape, jnp.bfloat16)
+    totals = pltpu.VMEM((1, all_width // DH, rows), jnp.float32)
     anywhere = pl.BlockSpec(memory_space=pl.ANY)
     low = functools.partial(pltpu.VMEM, dtype=jnp.bfloat16)
     wide = functools.partial(pltpu.VMEM, dtype=jnp.float32)
     copies = pltpu.SemaphoreType.DMA
-    return pl.pallas_call(
+    results = pl.pallas_call(
         functools.partial(kernel, group),
         name="spread_heads_attention",
         out_shape=(block, totals, block, block, block),
         in_specs=[pl.BlockSpec(memory_space=pltpu.SMEM)] + [anywhere] * 4,
-        out_specs=(anywhere,) * 5,
+        out_specs=(pl.BlockSpec(memory_space=pltpu.VMEM),) * 5,
         scratch_shapes=[
             low((RING, rows, group)),
             low((SPAN + RING, rows, group)),
@@ -377,9 +386,17 @@
             copies((1,)),
         ],
         compiler_params=pltpu.CompilerParams(
-            collective_id=0, has_side_effects=True, vmem_limit_bytes=56 * 2**20
+            collective_id=0, has_side_effects=True, vmem_limit_bytes=48 * 2**20
         ),
     )(lengths, queries, key_vectors, value_vectors, out_grad)
+    return pl.pallas_call(
+        write_out,
+        name="write_out",
+        out_shape=tuple(jax.ShapeDtypeStruct(r.shape, r.dtype) for r in results),
+        in_specs=[pl.BlockSpec(memory_space=pltpu.VMEM)] * 5,
+        out_specs=(anywhere,) * 5,
+        scratch_shapes=[copies((5,))],
+    )(*results)
 
 
 def solution(mesh):

time: 202 us -> 205 us (1.015)
  Pallas kernels: 191 us -> 198 us
  local copies, waits for them, and re-layouts: 9.88 us -> 5.9 us
    pallas_call x0 -> x1, Pallas kernels: none -> 6.86 us  [attend(): pl.pallas_call(write_out, name='write_out', out_shape=tuple((jax.ShapeDty...]
    unnamed x13 -> x10, local copies, waits for them, and re-layouts: 9.88 us -> 5.9 us
where the time goes in v2:
time: 205 us
  Pallas kernels  198 us (97%)
  local copies, waits for them, and re-layouts  5.9 us (3%)
    pallas_call x1, Pallas kernels, attend(): pl.pallas_call(functools.partial(kernel, group), name='spread_heads_atten...  191 us
    pallas_call x1, Pallas kernels, attend(): pl.pallas_call(write_out, name='write_out', out_shape=tuple((jax.ShapeDty...  6.86 us
    unnamed x10, local copies, waits for them, and re-layouts  5.9 us

profile of v2, /device:TPU:1, one launch (start us, length us, event | category | flops | bytes accessed | tf_op | source)
XLA Modules:
  0.0 204.7 jit_solution(1978506776205700025)
XLA Ops:
  0.6 191.3 %spread_heads_attention.1 = (bf16[1,128,8192]{2,1,0:T(8,128)(2,1)S(1)}, f32[1,64,128]{2,1,0:T(8,128)S(1)}, bf16[1,128,8192]{2,1,0:T(8,128)(2,1)S(1)}, bf16[1,128...) custom-call(s32[1,16]{1,0:T(1,128)} %lengths.1, bf16[1,128,8192]{2,1,0:T(8,128)(2,1)} %q_in.1, ...), custom_call_target="tpu_custom_call" | custom-call | tf_op jit(solution)/shard_map/spread_heads_attention/pallas_call | solution.py:351
  192.0 0.0 copy-start
  192.0 1.3 copy-done
  193.3 0.0 copy-start.1
  193.3 1.3 copy-done.1
  194.6 0.0 copy-start.2
  194.6 1.3 copy-done.2
  195.9 0.0 copy-start.3
  195.9 1.3 copy-done.3
  197.3 0.0 copy-start.4
  197.3 0.6 copy-done.4
  197.9 6.9 %write_out.1 = (bf16[1,128,8192]{2,1,0:T(8,128)(2,1)}, f32[1,64,128]{2,1,0:T(8,128)}, bf16[1,128,8192]{2,1,0:T(8,128)(2,1)}, bf16[1,128,8192]{2,1,0:T(8,128)(2,1)}, bf16[1,128,8192]{2,1,0:T(8,128)(2,1)}) custom-call(bf16[1,128,8192]{2,1,0:T(8,128)(2,1)} %copy-done, f32[1,64,128]{2,1,0:T(8,128)} %copy-done.4, bf16[1,128,8192]{2,1,0:T(8,128)(2,1)} %copy-done.1, ...), custom_call_target="tpu_custom_call" | custom-call | tf_op jit(solution)/shard_map/write_out/pallas_call | solution.py:392
Async XLA Ops:
  192.0 1.3 copy-start
  193.3 1.3 copy-start.1
  194.6 1.3 copy-start.2
  195.9 1.4 copy-start.3
  197.3 0.6 copy-start.4

commit v3 on v2

--- a/solution.py
+++ b/solution.py
@@ -338,6 +338,18 @@
         move.wait()
 
 
+def write_results(*results):
+    return pl.pallas_call(
+        write_out,
+        name="write_out",
+        out_shape=tuple(jax.ShapeDtypeStruct(r.shape, r.dtype) for r in results),
+        in_specs=[pl.BlockSpec(memory_space=pltpu.VMEM)] * 5,
+        out_specs=(pl.BlockSpec(memory_space=pl.ANY),) * 5,
+        scratch_shapes=[pltpu.SemaphoreType.DMA((5,))],
+        compiler_params=pltpu.CompilerParams(vmem_limit_bytes=2**20),
+    )(*(pltpu.with_memory_space_constraint(r, pltpu.VMEM) for r in results))
+
+
 def attend(queries, key_vectors, value_vectors, out_grad, lengths):
     _, rows, all_width = queries.shape
     group = all_width // RING
@@ -389,14 +401,7 @@
             collective_id=0, has_side_effects=True, vmem_limit_bytes=48 * 2**20
         ),
     )(lengths, queries, key_vectors, value_vectors, out_grad)
-    return pl.pallas_call(
-        write_out,
-        name="write_out",
-        out_shape=tuple(jax.ShapeDtypeStruct(r.shape, r.dtype) for r in results),
-        in_specs=[pl.BlockSpec(memory_space=pltpu.VMEM)] * 5,
-        out_specs=(anywhere,) * 5,
-        scratch_shapes=[copies((5,))],
-    )(*results)
+    return write_results(*results)
 
 
 def solution(mesh):

time: 205 us -> 195 us (0.951)
  local copies, waits for them, and re-layouts: 5.9 us -> 0 us
  Pallas kernels: 198 us -> 195 us
    unnamed x10 -> x0, local copies, waits for them, and re-layouts: 5.9 us -> none
    pallas_call x1, Pallas kernels: 6.86 us -> 3.39 us  [write_results(): pl.pallas_call(write_out, name='write_out', out_shape=tuple((jax.ShapeDty...]
where the time goes in v3:
time: 195 us
  Pallas kernels  195 us (100%)
    pallas_call x1, Pallas kernels, attend(): pl.pallas_call(functools.partial(kernel, group), name='spread_heads_atten...  191 us

profile of v3, /device:TPU:1, one launch (start us, length us, event | category | flops | bytes accessed | tf_op | source)
XLA Modules:
  0.0 195.3 jit_solution(11010858649639378876)
XLA Ops:
  0.6 191.3 %spread_heads_attention.1 = (bf16[1,128,8192]{2,1,0:T(8,128)(2,1)S(1)}, f32[1,64,128]{2,1,0:T(8,128)S(1)}, bf16[1,128,8192]{2,1,0:T(8,128)(2,1)S(1)}, bf16[1,128...) custom-call(s32[1,16]{1,0:T(1,128)} %lengths.1, bf16[1,128,8192]{2,1,0:T(8,128)(2,1)} %q_in.1, ...), custom_call_target="tpu_custom_call" | custom-call | tf_op jit(solution)/shard_map/spread_heads_attention/pallas_call | solution.py:363
  192.0 3.4 %write_out.1 = (bf16[1,128,8192]{2,1,0:T(8,128)(2,1)}, f32[1,64,128]{2,1,0:T(8,128)}, bf16[1,128,8192]{2,1,0:T(8,128)(2,1)}, bf16[1,128,8192]{2,1,0:T(8,128)(2,1)}, bf16[1,128,8192]{2,1,0:T(8,128)(2,1)}) custom-call(bf16[1,128,8192]{2,1,0:T(8,128)(2,1)S(1)} %get-tuple-element.10.refs_0_, f32[1,64,128]{2,1,0:T(8,128)S(1)} %get-tuple-element.11.refs_1_, ...), custom_call_target="tpu_custom_call" | custom-call | tf_op jit(solution)/shard_map/write_out/pallas_call | solution.py:342

commit v4 on v0

v4 whole, which is shorter than its diff:
```python
import functools

import jax
import jax.numpy as jnp
from jax import lax
from jax.experimental import pallas as pl
from jax.experimental.pallas import tpu as pltpu
from jax.sharding import PartitionSpec as P

DH = 128
ROWS = 128
HALF = 64
LONGEST = 384
COVER = LONGEST // 2
KEYS = COVER + ROWS
QUERIES = 3 * ROWS
HEADS = 2
AHEAD = 3
DEPTH = 1
PATIENCE = 1
TURN = DEPTH + PATIENCE + 1
LAG = TURN + DEPTH + AHEAD
SLOTS = AHEAD + 1
LOG2E = 1.4426950408889634
LN2 = 0.6931471805599453
MASKED = -1e30
NEVER = 1 << 30
MESH = pl.DeviceIdType.MESH

NT = (((1,), (1,)), ((), ()))
NN = (((1,), (0,)), ((), ()))
TN = (((0,), (0,)), ((), ()))


def dot(a, b, dims):
    return lax.dot_general(a, b, dims, preferred_element_type=jnp.float32)


def kernel(
    lengths,
    q_in,
    k_in,
    v_in,
    g_in,
    o_out,
    lse_out,
    dq_out,
    dk_out,
    dv_out,
    q_all,
    k_all,
    v_all,
    g_all,
    right1,
    right2,
    left1,
    left2,
    from_left1,
    from_left2,
    from_right1,
    from_right2,
    far_q1,
    far_q2,
    far_k1,
    far_k2,
    own_q,
    own_k,
    powers,
    pulls,
    peaks,
    stats,
    stats_left1,
    stats_left2,
    stats_right1,
    stats_right2,
    bias,
    in_local,
    msg_send,
    msg_recv,
    stat_send,
    stat_recv,
):
    width = HEADS * DH
    chunks = q_all.shape[1] // width
    steps = chunks + LAG
    spare = chunks + TURN
    blocks = lax.axis_size("ctx")
    dp = lax.axis_index("dp")
    me = lax.axis_index("ctx")

    def device(step):
        return (dp, (me + step + blocks) % blocks)

    def span(c):
        return pl.ds(pl.multiple_of(c * width, width), width)

    early = 8 * DH
    loads = [
        [
            pltpu.make_async_copy(source.at[0, :, part], kept.at[:, part], in_local.at[p, i])
            for i, (source, kept) in enumerate(
                ((k_in, k_all), (v_in, v_all), (q_in, q_all), (g_in, g_all))
            )
        ]
        for p, part in enumerate((slice(0, early), slice(early, q_all.shape[1])))
    ]
    for load in loads[0] + loads[1]:
        load.start()
    barrier = pltpu.get_barrier_semaphore()
    for step in (1, 2, -1, -2):
        pl.semaphore_signal(barrier, inc=1, device_id=device(step), device_id_type=MESH)

    last = blocks * ROWS

    def document_start(position):
        first = position * 0
        start = jnp.int32(0)
        for d in range(lengths.shape[1]):
            first = jnp.where(start <= position, start, first)
            start = start + lengths[0, d]
        return first

    def keys_cross(block):
        edge = block * ROWS
        return (edge - document_start(edge) <= COVER) | (edge >= last)

    keys0, keys1 = keys_cross(me), keys_cross(me + 1)

    for load in loads[0]:
        load.wait()
    pl.semaphore_wait(barrier, 4)

    routes = (
        (right1, from_left1, 1),
        (left1, from_right1, -1),
        (right2, from_left2, 1),
        (left2, from_right2, -1),
    )

    def message(s, i):
        staged, landed, step = routes[i]
        slot = s % SLOTS
        return pltpu.make_async_remote_copy(
            staged.at[slot],
            landed.at[s],
            msg_send.at[slot, i],
            msg_recv.at[s, i],
            device_id=device(step),
            device_id_type=MESH,
        )

    def start(s, which):
        for i in which:
            message(s, i).start()

    def reuse(s, which):
        @pl.when(s >= SLOTS)
        def _():
            for i in which:
                message(s - SLOTS, i).wait_send()

    def send_blocks(s):
        slot = s % SLOTS
        columns = span(jnp.minimum(s, chunks - 1))
        keep = (s + 3 * LAG) % 4
        back = jnp.where(s >= LAG, s - LAG + TURN, spare)
        reuse(s, (0, 1))
        for a, (own_key, own_query) in enumerate(((k_all, q_all), (v_all, g_all))):
            more = from_left2[back, a].astype(jnp.float32)
            more = jnp.where(keys0, 0.0, more)
            head = (far_q1[keep, a, :HALF] + more).astype(jnp.bfloat16)
            tail = far_q1[keep, a, HALF:].astype(jnp.bfloat16)
            right1[slot, a, :HALF] = jnp.where(keys1, own_key[:HALF, columns], head)
            right1[slot, a, HALF:] = jnp.where(keys1, own_key[HALF:, columns], tail)
            more = from_right2[back, a].astype(jnp.float32)
            more = jnp.where(keys1, more, 0.0)
            head = far_k1[keep, a, :HALF].astype(jnp.bfloat16)
            tail = (far_k1[keep, a, HALF:] + more).astype(jnp.bfloat16)
            left1[slot, a, :HALF] = jnp.where(keys0, head, own_query[:HALF, columns])
            left1[slot, a, HALF:] = jnp.where(keys0, tail, own_query[HALF:, columns])
        start(s, (0, 1))

    def send_halves(s):
        slot = s % SLOTS
        done = (s + TURN) % 2
        reuse(s, (2, 3))
        for a in range(2):
            right2[slot, a] = jnp.where(keys1, from_left1[s, a, ROWS - HALF :], far_q2[done, a])
            left2[slot, a] = jnp.where(keys0, far_k2[done, a], from_right1[s, a, :HALF])
        start(s, (2, 3))

    stat_routes = (
        (slice(ROWS, 3 * ROWS), stats_left1, 1),
        (slice(0, 2 * ROWS), stats_right1, -1),
        (slice(2 * ROWS, 3 * ROWS), stats_left2, 2),
        (slice(0, ROWS), stats_right2, -2),
    )

    def stat_message(c, i):
        lanes, landed, step = stat_routes[i]
        return pltpu.make_async_remote_copy(
            stats.at[c, :, lanes],
            landed.at[c],
            stat_send.at[c, i],
            stat_recv.at[c, i],
            device_id=device(step),
            device_id_type=MESH,
        )

    scale = DH ** (-0.5)
    pad = jnp.zeros((ROWS - HALF, DH), jnp.bfloat16)

    def met_keys(c, a, h):
        inner = slice(h * DH, (h + 1) * DH)
        own = (k_all, v_all)[a][:, pl.ds(pl.multiple_of(c * width + h * DH, DH), DH)]
        return jnp.concatenate(
            [from_left2[c, a, :, inner], from_left1[c, a, :, inner], own], axis=0
        )

    def met_queries(c, a, h):
        inner = slice(h * DH, (h + 1) * DH)
        own = (q_all, g_all)[a][:, pl.ds(pl.multiple_of(c * width + h * DH, DH), DH)]
        return jnp.concatenate(
            [own, from_right1[c, a, :, inner], from_right2[c, a, :, inner], pad], axis=0
        )

    def partial_totals(c):
        slot = c % (PATIENCE + 1)
        for h in range(HEADS):
            score = dot(met_keys(c, 0, h), met_queries(c, 0, h), NT) * (scale * LOG2E) + bias[...]
            pull = dot(met_keys(c, 1, h), met_queries(c, 1, h), NT)
            pulls[slot, h] = pull
            peak = jnp.max(score, axis=0, keepdims=True)
            power = jnp.exp2(score - peak)
            powers[slot, h] = power
            peaks[slot, pl.ds(h, 1), :] = peak
            total = jnp.sum(power, axis=0, keepdims=True)
            along = jnp.sum(power * pull, axis=0, keepdims=True) / total
            stats[c, pl.ds(2 * h, 1), :] = peak + jnp.log2(total)
            stats[c, pl.ds(2 * h + 1, 1), :] = along
        for i in range(4):
            stat_message(c, i).start()

    def gradients(c):
        slot, done = c % (PATIENCE + 1), c % 2
        keep, turn = c % 8, c % 4
        for i in range(4):
            stat_message(c, i).wait_recv()
        mine = stats[c]
        left, right = stats_left1[c], stats_right1[c]
        second = jnp.concatenate([left, right[:, ROWS:]], axis=1)
        third = jnp.concatenate([stats_left2[c], right[:, :ROWS], stats_right2[c]], axis=1)
        for h in range(HEADS):
            inner = slice(h * DH, (h + 1) * DH)
            logs = [part[2 * h : 2 * h + 1] for part in (mine, second, third)]
            peak = jnp.maximum(jnp.maximum(logs[0], logs[1]), logs[2])
            shares = [jnp.exp2(log - peak) for log in logs]
            total = shares[0] + shares[1] + shares[2]
            log_total = peak + jnp.log2(total)
            along = sum(
                share * part[2 * h + 1 : 2 * h + 2]
                for share, part in zip(shares, (mine, second, third))
            ) / total
            lse_out[0, pl.ds(c * HEADS + h, 1), :] = log_total[:, :ROWS] * LN2
            weight = powers[slot, h] * jnp.exp2(peaks[slot, pl.ds(h, 1), :] - log_total)
            slope = (weight * (pulls[slot, h] - along)).astype(jnp.bfloat16)
            weight = weight.astype(jnp.bfloat16)
            keys, values = met_keys(c, 0, h), met_keys(c, 1, h)
            queries, grads = met_queries(c, 0, h), met_queries(c, 1, h)
            for a, (query_part, key_part) in enumerate(
                (
                    (dot(weight, values, TN), dot(slope, queries, NN) * scale),
                    (dot(slope, keys, TN) * scale, dot(weight, grads, NN)),
                )
            ):
                own_q[keep, a, :, inner] = query_part[:ROWS]
                far_q1[turn, a, :, inner] = query_part[ROWS : 2 * ROWS]
                far_q2[done, a, :, inner] = query_part[2 * ROWS : 2 * ROWS + HALF].astype(
                    jnp.bfloat16
                )
                own_k[keep, a, :, inner] = key_part[COVER:]
                far_k1[turn, a, :, inner] = key_part[HALF:COVER]
                far_k2[done, a, :, inner] = key_part[:HALF].astype(jnp.bfloat16)

    def finish(s):
        c = s - LAG
        keep = c % 8
        columns = span(c)
        for a, (query_out, key_out) in enumerate(((o_out, dk_out), (dq_out, dv_out))):
            query_part = jnp.where(keys0, 0.0, from_left1[s, a].astype(jnp.float32))
            query_out[0, :, columns] = (own_q[keep, a] + query_part).astype(jnp.bfloat16)
            key_part = jnp.where(keys1, from_right1[s, a].astype(jnp.float32), 0.0)
            key_out[0, :, columns] = (own_k[keep, a] + key_part).astype(jnp.bfloat16)

    for far in (far_q1, far_q2, far_k1, far_k2):
        far[...] = jnp.zeros(far.shape, far.dtype)
    for landed in (from_left2, from_right2):
        landed[spare] = jnp.zeros(landed.shape[1:], landed.dtype)
    for s in range(AHEAD):
        send_blocks(s)

    query_pos = me * ROWS + lax.broadcasted_iota(jnp.int32, (1, QUERIES), 1)
    first = document_start(query_pos)
    lane = lax.broadcasted_iota(jnp.int32, (1, QUERIES), 1)
    first = jnp.where((query_pos >= last) | (lane >= 2 * ROWS + HALF), NEVER, first)
    first = jnp.where((lane >= ROWS) & (lane * 0 + keys1.astype(jnp.int32) > 0), NEVER, first)
    key_pos = me * ROWS - COVER + lax.broadcasted_iota(jnp.int32, (KEYS, 1), 0)
    seen_pos = jnp.where(
        (key_pos < me * ROWS) & (key_pos * 0 + keys0.astype(jnp.int32) == 0), -1, key_pos
    )
    bias[...] = jnp.where((seen_pos >= first) & (key_pos <= query_pos), 0.0, MASKED)

    for load in loads[1]:
        load.wait()

    def one_step(s, carry):
        for i in (0, 1):
            message(s, i).wait_recv()

        @pl.when(s < chunks + TURN)
        def _():
            send_halves(s)

        @pl.when((s >= DEPTH) & (s < chunks + TURN + DEPTH))
        def _():
            for i in (2, 3):
                message(s - DEPTH, i).wait_recv()

        @pl.when((s >= DEPTH) & (s < chunks + DEPTH))
        def _():
            partial_totals(s - DEPTH)

        @pl.when(s + AHEAD < steps)
        def _():
            send_blocks(s + AHEAD)

        @pl.when((s >= DEPTH + PATIENCE) & (s < chunks + DEPTH + PATIENCE))
        def _():
            gradients(s - DEPTH - PATIENCE)

        @pl.when(s >= LAG)
        def _():
            finish(s)

        return carry

    lax.fori_loop(0, steps, one_step, 0)
    for which, count in (((0, 1), steps), ((2, 3), chunks + TURN)):
        for s in range(count - SLOTS, count):
            for i in which:
                message(s, i).wait_send()

    def drain(c, carry):
        for i in range(4):
            stat_message(c, i).wait_send()
        return carry

    lax.fori_loop(0, chunks, drain, 0)


def write_out(*refs):
    sems = refs[10]
    moves = [pltpu.make_async_copy(refs[i], refs[5 + i], sems.at[i]) for i in range(5)]
    for move in moves:
        move.start()
    for move in moves:
        move.wait()


def write_results(*results):
    return pl.pallas_call(
        write_out,
        name="write_out",
        out_shape=tuple(jax.ShapeDtypeStruct(r.shape, r.dtype) for r in results),
        in_specs=[pl.BlockSpec(memory_space=pltpu.VMEM)] * 5,
        out_specs=(pl.BlockSpec(memory_space=pl.ANY),) * 5,
        scratch_shapes=[pltpu.SemaphoreType.DMA((5,))],
        compiler_params=pltpu.CompilerParams(vmem_limit_bytes=2**20),
    )(*(pltpu.with_memory_space_constraint(r, pltpu.VMEM) for r in results))


def attend(queries, key_vectors, value_vectors, out_grad, lengths):
    _, rows, all_width = queries.shape
    heads = all_width // DH
    width = HEADS * DH
    chunks = heads // HEADS
    steps = chunks + LAG
    block = pltpu.VMEM(queries.shape, jnp.bfloat16)
    totals = pltpu.VMEM((1, heads, rows), jnp.float32)
    anywhere = pl.BlockSpec(memory_space=pl.ANY)
    low = functools.partial(pltpu.VMEM, dtype=jnp.bfloat16)
    wide = functools.partial(pltpu.VMEM, dtype=jnp.float32)
    copies = pltpu.SemaphoreType.DMA
    results = pl.pallas_call(
        kernel,
        name="chain_attention",
        out_shape=(block, totals, block, block, block),
        in_specs=[pl.BlockSpec(memory_space=pltpu.SMEM)] + [anywhere] * 4,
        out_specs=(pl.BlockSpec(memory_space=pltpu.VMEM),) * 5,
        scratch_shapes=[low((rows, all_width))] * 4
        + [low((SLOTS, 2, ROWS, width)), low((SLOTS, 2, HALF, width))] * 2
        + [low((steps, 2, ROWS, width)), low((chunks + TURN + 1, 2, HALF, width))] * 2
        + [wide((4, 2, ROWS, width)), low((2, 2, HALF, width))] * 2
        + [
            wide((8, 2, ROWS, width)),
            wide((8, 2, ROWS, width)),
            wide((PATIENCE + 1, HEADS, KEYS, QUERIES)),
            wide((PATIENCE + 1, HEADS, KEYS, QUERIES)),
            wide((PATIENCE + 1, HEADS, QUERIES)),
            wide((chunks, 2 * HEADS, QUERIES)),
            wide((chunks, 2 * HEADS, 2 * ROWS)),
            wide((chunks, 2 * HEADS, ROWS)),
            wide((chunks, 2 * HEADS, 2 * ROWS)),
            wide((chunks, 2 * HEADS, ROWS)),
            wide((KEYS, QUERIES)),
            copies((2, 4)),
            copies((SLOTS, 4)),
            copies((steps, 4)),
            copies((chunks, 4)),
            copies((chunks, 4)),
        ],
        compiler_params=pltpu.CompilerParams(
            collective_id=0, has_side_effects=True, vmem_limit_bytes=48 * 2**20
        ),
    )(lengths, queries, key_vectors, value_vectors, out_grad)
    return write_results(*results)


def solution(mesh):
    block = P("dp", "ctx", None)
    in_specs = (block, block, block, block, P("dp", None))
    out_specs = (block, P("dp", None, "ctx"), block, block, block)
    return jax.shard_map(attend, mesh=mesh, in_specs=in_specs, out_specs=out_specs, check_vma=False)
```

time: 1040 us -> 185 us (0.18)
  the two profiles are of different devices: /device:TPU:32 before, /device:TPU:1 now
where the time goes in v4:
time: 185 us; the launch traced here: 182 us
  Pallas kernels  182 us (98%)
    pallas_call x1, Pallas kernels, attend(): pl.pallas_call(kernel, name='chain_attention', out_shape=(block, totals,...  178 us

profile of v4, /device:TPU:1, one launch (start us, length us, event | category | flops | bytes accessed | tf_op | source)
XLA Modules:
  0.0 182.4 jit_solution(12230893321810772075)
XLA Ops:
  0.6 178.4 %chain_attention.1 = (bf16[1,128,8192]{2,1,0:T(8,128)(2,1)S(1)}, f32[1,64,128]{2,1,0:T(8,128)S(1)}, bf16[1,128,8192]{2,1,0:T(8,128)(2,1)S(1)}, bf16[1,128,8192]{...) custom-call(s32[1,16]{1,0:T(1,128)} %lengths.1, bf16[1,128,8192]{2,1,0:T(8,128)(2,1)} %q_in.1, bf16[1,128,8192]{2,1,0:T(8,128)(2,1)} %k_in.1, ...), custom_call_target="tpu_custom_call" | custom-call | tf_op jit(solution)/shard_map/chain_attention/pallas_call | solution.py:394
  179.0 3.4 %write_out.1 = (bf16[1,128,8192]{2,1,0:T(8,128)(2,1)}, f32[1,64,128]{2,1,0:T(8,128)}, bf16[1,128,8192]{2,1,0:T(8,128)(2,1)}, bf16[1,128,8192]{2,1,0:T(8,128)(2,1)}, bf16[1,128,8192]{2,1,0:T(8,128)(2,1)}) custom-call(bf16[1,128,8192]{2,1,0:T(8,128)(2,1)S(1)} %get-tuple-element.10.refs_0_, f32[1,64,128]{2,1,0:T(8,128)S(1)} %get-tuple-element.11.refs_1_, ...), custom_call_target="tpu_custom_call" | custom-call | tf_op jit(solution)/shard_map/write_out/pallas_call | solution.py:371

commit v5 on v4

--- a/solution.py
+++ b/solution.py
@@ -69,6 +69,10 @@
     pulls,
     peaks,
     stats,
+    to_left1,
+    to_left2,
+    to_right1,
+    to_right2,
     stats_left1,
     stats_left2,
     stats_right1,
@@ -190,21 +194,32 @@
         start(s, (2, 3))
 
     stat_routes = (
-        (slice(ROWS, 3 * ROWS), stats_left1, 1),
-        (slice(0, 2 * ROWS), stats_right1, -1),
-        (slice(2 * ROWS, 3 * ROWS), stats_left2, 2),
-        (slice(0, ROWS), stats_right2, -2),
+        (to_right1, stats_left1, 1),
+        (to_left1, stats_right1, -1),
+        (to_right2, stats_left2, 2),
+        (to_left2, stats_right2, -2),
     )
 
     def stat_message(c, i):
-        lanes, landed, step = stat_routes[i]
+        staged, landed, step = stat_routes[i]
         return pltpu.make_async_remote_copy(
-            stats.at[c, :, lanes],
+            staged.at[c],
             landed.at[c],
             stat_send.at[c, i],
             stat_recv.at[c, i],
             device_id=device(step),
             device_id_type=MESH,
+        )
+
+    def halves(log, along, first):
+        part = slice(first, first + HALF)
+        return jnp.concatenate([log[:, part], along[:, part]], axis=1)
+
+    def unpack(row, fill):
+        rest = jnp.full((1, ROWS - HALF), fill, jnp.float32)
+        return (
+            jnp.concatenate([row[:, :HALF], rest], axis=1),
+            jnp.concatenate([row[:, HALF:], jnp.zeros_like(rest)], axis=1),
         )
 
     scale = DH ** (-0.5)
@@ -236,8 +251,18 @@
             peaks[slot, pl.ds(h, 1), :] = peak
             total = jnp.sum(power, axis=0, keepdims=True)
             along = jnp.sum(power * pull, axis=0, keepdims=True) / total
-            stats[c, pl.ds(2 * h, 1), :] = peak + jnp.log2(total)
-            stats[c, pl.ds(2 * h + 1, 1), :] = along
+            log = peak + jnp.log2(total)
+            stats[slot, pl.ds(2 * h, 1), :] = log
+            stats[slot, pl.ds(2 * h + 1, 1), :] = along
+            for one, two, first, second in (
+                (to_left1, to_left2, 0, ROWS),
+                (to_right1, to_right2, ROWS, 2 * ROWS),
+            ):
+                one[c, pl.ds(3 * h, 1), :] = log[:, first : first + ROWS]
+                one[c, pl.ds(3 * h + 1, 1), :] = along[:, first : first + ROWS]
+                one[c, pl.ds(3 * h + 2, 1), :] = halves(log, along, second)
+            to_left2[c, pl.ds(h, 1), :] = halves(log, along, 0)
+            to_right2[c, pl.ds(h, 1), :] = halves(log, along, 2 * ROWS)
         for i in range(4):
             stat_message(c, i).start()
 
@@ -245,22 +270,33 @@
         slot, done = c % (PATIENCE + 1), c % 2
         keep, turn = c % 8, c % 4
         for i in range(4):
-            stat_message(c, i).wait_recv()
-        mine = stats[c]
-        left, right = stats_left1[c], stats_right1[c]
-        second = jnp.concatenate([left, right[:, ROWS:]], axis=1)
-        third = jnp.concatenate([stats_left2[c], right[:, :ROWS], stats_right2[c]], axis=1)
+            stat_message(c, i).wait()
+        mine = stats[slot]
+        left1, right1, left2, right2 = (
+            landed[c] for landed in (stats_left1, stats_right1, stats_left2, stats_right2)
+        )
         for h in range(HEADS):
             inner = slice(h * DH, (h + 1) * DH)
-            logs = [part[2 * h : 2 * h + 1] for part in (mine, second, third)]
+            near, far = 3 * h, slice(3 * h + 2, 3 * h + 3)
+            left_log, left_along = unpack(left1[far], MASKED)
+            right_log, right_along = unpack(right1[far], 0.0)
+            left2_log, left2_along = unpack(left2[h : h + 1], MASKED)
+            right2_log, right2_along = unpack(right2[h : h + 1], 0.0)
+            logs = [
+                mine[2 * h : 2 * h + 1],
+                jnp.concatenate([left1[near : near + 1], left_log, right_log], axis=1),
+                jnp.concatenate([left2_log, right1[near : near + 1], right2_log], axis=1),
+            ]
+            alongs = [
+                mine[2 * h + 1 : 2 * h + 2],
+                jnp.concatenate([left1[near + 1 : near + 2], left_along, right_along], axis=1),
+                jnp.concatenate([left2_along, right1[near + 1 : near + 2], right2_along], axis=1),
+            ]
             peak = jnp.maximum(jnp.maximum(logs[0], logs[1]), logs[2])
             shares = [jnp.exp2(log - peak) for log in logs]
             total = shares[0] + shares[1] + shares[2]
             log_total = peak + jnp.log2(total)
-            along = sum(
-                share * part[2 * h + 1 : 2 * h + 2]
-                for share, part in zip(shares, (mine, second, third))
-            ) / total
+            along = sum(share * part for share, part in zip(shares, alongs)) / total
             lse_out[0, pl.ds(c * HEADS + h, 1), :] = log_total[:, :ROWS] * LN2
             weight = powers[slot, h] * jnp.exp2(peaks[slot, pl.ds(h, 1), :] - log_total)
             slope = (weight * (pulls[slot, h] - along)).astype(jnp.bfloat16)
@@ -349,13 +385,6 @@
         for s in range(count - SLOTS, count):
             for i in which:
                 message(s, i).wait_send()
-
-    def drain(c, carry):
-        for i in range(4):
-            stat_message(c, i).wait_send()
-        return carry
-
-    lax.fori_loop(0, chunks, drain, 0)
 
 
 def write_out(*refs):
@@ -407,11 +436,10 @@
             wide((PATIENCE + 1, HEADS, KEYS, QUERIES)),
             wide((PATIENCE + 1, HEADS, KEYS, QUERIES)),
             wide((PATIENCE + 1, HEADS, QUERIES)),
-            wide((chunks, 2 * HEADS, QUERIES)),
-            wide((chunks, 2 * HEADS, 2 * ROWS)),
-            wide((chunks, 2 * HEADS, ROWS)),
-            wide((chunks, 2 * HEADS, 2 * ROWS)),
-            wide((chunks, 2 * HEADS, ROWS)),
+            wide((PATIENCE + 1, 2 * HEADS, QUERIES)),
+        ]
+        + [wide((chunks, 3 * HEADS, ROWS)), wide((chunks, HEADS, ROWS))] * 4
+        + [
             wide((KEYS, QUERIES)),
             copies((2, 4)),
             copies((SLOTS, 4)),

time: 185 us -> 182 us (0.984)
  Pallas kernels: 182 us -> 179 us
    pallas_call x1, Pallas kernels: 178 us -> 176 us  [attend(): pl.pallas_call(kernel, name='chain_attention', out_shape=(block, totals,...]
where the time goes in v5:
time: 182 us; the launch traced here: 180 us
  Pallas kernels  179 us (98%)
    pallas_call x1, Pallas kernels, attend(): pl.pallas_call(kernel, name='chain_attention', out_shape=(block, totals,...  176 us

profile of v5, /device:TPU:1, one launch (start us, length us, event | category | flops | bytes accessed | tf_op | source)
XLA Modules:
  0.0 180.0 jit_solution(14261526289005823008)
XLA Ops:
  0.6 176.0 %chain_attention.1 = (bf16[1,128,8192]{2,1,0:T(8,128)(2,1)S(1)}, f32[1,64,128]{2,1,0:T(8,128)S(1)}, bf16[1,128,8192]{2,1,0:T(8,128)(2,1)S(1)}, bf16[1,128,8192]{...) custom-call(s32[1,16]{1,0:T(1,128)} %lengths.1, bf16[1,128,8192]{2,1,0:T(8,128)(2,1)} %q_in.1, bf16[1,128,8192]{2,1,0:T(8,128)(2,1)} %k_in.1, ...), custom_call_target="tpu_custom_call" | custom-call | tf_op jit(solution)/shard_map/chain_attention/pallas_call | solution.py:423
  176.6 3.4 %write_out.1 = (bf16[1,128,8192]{2,1,0:T(8,128)(2,1)}, f32[1,64,128]{2,1,0:T(8,128)}, bf16[1,128,8192]{2,1,0:T(8,128)(2,1)}, bf16[1,128,8192]{2,1,0:T(8,128)(2,1)}, bf16[1,128,8192]{2,1,0:T(8,128)(2,1)}) custom-call(bf16[1,128,8192]{2,1,0:T(8,128)(2,1)S(1)} %get-tuple-element.10.refs_0_, f32[1,64,128]{2,1,0:T(8,128)S(1)} %get-tuple-element.11.refs_1_, ...), custom_call_target="tpu_custom_call" | custom-call | tf_op jit(solution)/shard_map/write_out/pallas_call | solution.py:400

commit v6 on v5

--- a/solution.py
+++ b/solution.py
@@ -15,12 +15,13 @@
 KEYS = COVER + ROWS
 QUERIES = 3 * ROWS
 HEADS = 2
-AHEAD = 3
+AHEAD = 2
 DEPTH = 1
 PATIENCE = 1
 TURN = DEPTH + PATIENCE + 1
 LAG = TURN + DEPTH + AHEAD
 SLOTS = AHEAD + 1
+TOGETHER = 1
 LOG2E = 1.4426950408889634
 LN2 = 0.6931471805599453
 MASKED = -1e30
@@ -83,6 +84,7 @@
     msg_recv,
     stat_send,
     stat_recv,
+    pair,
 ):
     width = HEADS * DH
     chunks = q_all.shape[1] // width
@@ -113,6 +115,8 @@
     barrier = pltpu.get_barrier_semaphore()
     for step in (1, 2, -1, -2):
         pl.semaphore_signal(barrier, inc=1, device_id=device(step), device_id_type=MESH)
+    partner = (dp + 1 - 2 * (dp % 2), me)
+    pl.semaphore_signal(barrier, inc=1, device_id=partner, device_id_type=MESH)
 
     last = blocks * ROWS
 
@@ -132,7 +136,7 @@
 
     for load in loads[0]:
         load.wait()
-    pl.semaphore_wait(barrier, 4)
+    pl.semaphore_wait(barrier, 5)
 
     routes = (
         (right1, from_left1, 1),
@@ -350,6 +354,12 @@
         load.wait()
 
     def one_step(s, carry):
+        pl.semaphore_signal(pair, inc=1, device_id=partner, device_id_type=MESH)
+
+        @pl.when(s >= TOGETHER)
+        def _():
+            pl.semaphore_wait(pair, 1)
+
         for i in (0, 1):
             message(s, i).wait_recv()
 
@@ -381,6 +391,7 @@
         return carry
 
     lax.fori_loop(0, steps, one_step, 0)
+    pl.semaphore_wait(pair, TOGETHER)
     for which, count in (((0, 1), steps), ((2, 3), chunks + TURN)):
         for s in range(count - SLOTS, count):
             for i in which:
@@ -446,6 +457,7 @@
             copies((steps, 4)),
             copies((chunks, 4)),
             copies((chunks, 4)),
+            pltpu.SemaphoreType.REGULAR,
         ],
         compiler_params=pltpu.CompilerParams(
             collective_id=0, has_side_effects=True, vmem_limit_bytes=48 * 2**20

time: 182 us -> 182 us (level)
  no operation moved by 1% of the time
where the time goes in v6:
time: 182 us; the launch traced here: 179 us
  Pallas kernels  178 us (98%)
    pallas_call x1, Pallas kernels, attend(): pl.pallas_call(kernel, name='chain_attention', out_shape=(block, totals,...  175 us

profile of v6, /device:TPU:1, one launch (start us, length us, event | category | flops | bytes accessed | tf_op | source)
XLA Modules:
  0.0 178.7 jit_solution(11716880195800174031)
XLA Ops:
  0.6 174.7 %chain_attention.1 = (bf16[1,128,8192]{2,1,0:T(8,128)(2,1)S(1)}, f32[1,64,128]{2,1,0:T(8,128)S(1)}, bf16[1,128,8192]{2,1,0:T(8,128)(2,1)S(1)}, bf16[1,128,8192]{...) custom-call(s32[1,16]{1,0:T(1,128)} %lengths.1, bf16[1,128,8192]{2,1,0:T(8,128)(2,1)} %q_in.1, bf16[1,128,8192]{2,1,0:T(8,128)(2,1)} %k_in.1, ...), custom_call_target="tpu_custom_call" | custom-call | tf_op jit(solution)/shard_map/chain_attention/pallas_call | solution.py:434
  175.3 3.4 %write_out.1 = (bf16[1,128,8192]{2,1,0:T(8,128)(2,1)}, f32[1,64,128]{2,1,0:T(8,128)}, bf16[1,128,8192]{2,1,0:T(8,128)(2,1)}, bf16[1,128,8192]{2,1,0:T(8,128)(2,1)}, bf16[1,128,8192]{2,1,0:T(8,128)(2,1)}) custom-call(bf16[1,128,8192]{2,1,0:T(8,128)(2,1)S(1)} %get-tuple-element.10.refs_0_, f32[1,64,128]{2,1,0:T(8,128)S(1)} %get-tuple-element.11.refs_1_, ...), custom_call_target="tpu_custom_call" | custom-call | tf_op jit(solution)/shard_map/write_out/pallas_call | solution.py:411
